TPU v7x, 256 devices: a whole 4x4x8 slice. The times are simulated.
256 devices in a mesh: dp: 16 (over z, core), tensor: 16 (over y, x).
Axes of the slice: x: 4, y: 4, z: 8, core: 2. Of those that a mesh axis runs over, the one named last changes fastest.
Arguments:
- tokens: bfloat16 [8192, 8192], P('dp', 'tensor'), may hold values from -6 to 6
- weight: bfloat16 [8192, 8192], P('tensor'), may hold values from -0.0625 to 0.0625
- down_adapter: bfloat16 [8192, 16], P('tensor'), may hold values from -0.0625 to 0.0625
- up_adapter: bfloat16 [16, 8192], replicated, may hold values from -0.29882812 to 0.29882812
- cotangent: bfloat16 [8192, 8192], P(('dp', 'tensor')), may hold values from -6 to 6
Outputs:
- output: bfloat16 [8192, 8192], P(('dp', 'tensor'))
- token_gradient: bfloat16 [8192, 8192], P('dp', 'tensor')
- grad_a: float32 [8192, 16], P('tensor')
- grad_b: float32 [16, 8192], replicated
All inputs are finite; a program needn't handle non-finite values.
Results may differ from a plain program's by a relative error of at most 0.0029.
Values may be sent and summed in bfloat16 or wider, within the bound.
A program may use at most 128 MiB of HBM per device.

v0:
```python
import math

import jax
import jax.numpy as jnp
from jax import lax
from jax.sharding import PartitionSpec as P

adapter_scale = 0.5


def contract_trailing(left, right):
    return lax.dot_general(
        left, right, (((1,), (1,)), ((), ())), preferred_element_type=jnp.float32
    )


def contract_first(left, right):
    return lax.dot_general(
        left, right, (((0,), (0,)), ((), ())), preferred_element_type=jnp.float32
    )


def per_device(tokens, weight, down_adapter, up_adapter, cotangent):
    low_part = jnp.dot(tokens, down_adapter, preferred_element_type=jnp.float32)
    partial_value = jnp.dot(tokens, weight, preferred_element_type=jnp.float32)
    frozen_output, lowrank_sum = (
        lax.psum_scatter(partial_value, "tensor", scatter_dimension=0, tiled=True),
        lax.psum_scatter(low_part, "tensor", scatter_dimension=0, tiled=True),
    )
    adapted_output = lowrank_sum.astype(jnp.bfloat16)
    output = (
        frozen_output
        + adapter_scale * jnp.dot(adapted_output, up_adapter, preferred_element_type=jnp.float32)
    ).astype(jnp.bfloat16)
    low_rows = contract_trailing(cotangent, up_adapter).astype(jnp.bfloat16)
    full_rows, narrow_gradient = (
        lax.all_gather(cotangent, "tensor", axis=0, tiled=True),
        lax.all_gather(low_rows, "tensor", axis=0, tiled=True),
    )
    frozen_gradient = contract_trailing(full_rows, weight)
    token_gradient = (
        frozen_gradient + adapter_scale * contract_trailing(narrow_gradient, down_adapter)
    ).astype(jnp.bfloat16)
    every_token = tokens.shape[0] * lax.axis_size("dp")
    gradient_factor = adapter_scale / math.sqrt(every_token)
    first_part = contract_first(tokens, narrow_gradient)
    second_part = contract_first(adapted_output, cotangent)
    first_sum = lax.psum(first_part, "dp")
    second_sum = lax.psum(second_part, ("dp", "tensor"))
    return (output, token_gradient, gradient_factor * first_sum, gradient_factor * second_sum)


def solution(mesh):
    placed = (
        P("dp", "tensor"),
        P("tensor", None),
        P("tensor", None),
        P(),
        P(("dp", "tensor"), None),
    )
    return jax.shard_map(
        per_device,
        mesh=mesh,
        in_specs=placed,
        out_specs=(P(("dp", "tensor"), None), P("dp", "tensor"), P("tensor", None), P()),
        check_vma=False,
    )
```

profile of v0, /device:TPU:1, one launch (start us, length us, event | category | flops | bytes accessed | tf_op | source)
XLA Modules:
  0.0 556.7 jit_solution(6430244104369024675)
XLA Ops:
  7.2 0.0 copy-start
  7.2 0.0 reduce-scatter.7.cloned.1.call-start
  7.2 1.0 copy-done
  8.2 1.7 fusion.9
  9.9 0.0 reduce-scatter.7.cloned.1.call-update
  9.9 0.0 all-reduce.2.cloned.1.call-start
  10.0 81.3 %reduce-scatter.7.cloned.1.call-done = f32[32,16]{1,0:T(8,128)} async-done(((f32[512,16]{1,0:T(8,128)}), f32[32,16]{1,0:T(8,128)}) %reduce-scatter.7.cloned.1.call-update) | async-done | bytes 2064
  91.3 0.8 copy.12
  92.1 2.1 fusion.11
  94.1 0.0 all-reduce.2.cloned.1.call-update
  94.2 0.0 all-gather.3.cloned.1.call-start
  94.2 0.7 all-gather.3.cloned.1.call-update
  94.9 0.0 reduce-scatter.5.cloned.1.call-start
  94.9 11.5 %fusion.8 = f32[512,8192]{1,0:T(8,128)} fusion(bf16[512,512]{1,0:T(8,128)(2,1)S(1)} %copy-done, bf16[512,8192]{1,0:T(8,128)(2,1)} %param.6), kind=kOutput, calls=%fused_computation.14 | convolution fusion | flops 4294967296 | bytes 25690112 | tf_op jit(solution)/shard_map/dot_general | solution.py:25
  106.4 0.0 copy-start.1
  106.4 0.0 reduce-scatter.5.cloned.1.call-update
  106.4 1.0 copy-done.1
  107.5 0.1 copy-done.2
  107.5 0.2 fusion.4
  107.8 17.4 %all-gather = bf16[16,32,16]{1,2,0:T(8,128)(2,1)S(1)} all-gather(bf16[1,32,16]{1,2,0:T(8,128)(2,1)S(1)} %fusion.4), channel_id=1, replica_groups=mesh['dp'=16,'tensor'=16] {'tensor'}, dimensions={0}, use_global_device_ids=true | all-gather | bytes 17408 | tf_op jit(solution)/shard_map/all_gather | solution.py:38
  125.2 0.1 reshape.9
  125.3 0.2 convolution_bitcast_fusion
  125.5 51.0 %psum.14 = f32[512,16]{0,1:T(8,128)S(1)} all-reduce(f32[512,16]{0,1:T(8,128)S(1)} %convolution_bitcast_fusion), channel_id=1, replica_groups=mesh['dp'=16,'tensor'=16] {'dp'}, use_global_device_ids=true, to_apply=%region_2.0 | all-reduce | flops 8192 | bytes 65536 | tf_op jit(solution)/shard_map/psum | solution.py:48
  176.5 0.6 broadcast_multiply_fusion.1
  177.1 173.0 %all-reduce.2.cloned.1.call-done = f32[16,8192]{1,0:T(8,128)} async-done(((f32[16,8192]{1,0:T(8,128)}), f32[16,8192]{1,0:T(8,128)}) %all-reduce.2.cloned.1.call-update) | async-done | bytes 524304 | tf_op jit(solution)/shard_map/psum | solution.py:49
  350.1 1.9 broadcast_multiply_fusion
  351.9 76.8 %all-gather.3.cloned.1.call-done = bf16[512,8192]{1,0:T(8,128)(2,1)} async-done(((bf16[32,8192]{1,0:T(8,128)(2,1)}), bf16[512,8192]{1,0:T(8,128)(2,1)}) %all-gather.3.cloned.1.call-update) | async-done | bytes 8388624 | tf_op jit(solution)/shard_map/all_gather | solution.py:37
  428.8 9.5 %fusion.10 = f32[512,512]{1,0:T(8,128)S(1)} fusion(bf16[512,8192]{1,0:T(8,128)(2,1)} %all-gather.3.cloned.1.call-done, bf16[512,8192]{1,0:T(8,128)(2,1)} %param.6), kind=kOutput, calls=%fused_computation.16 | convolution fusion | flops 4294967296 | bytes 17825792 | tf_op jit(solution)/shard_map/dot_general | solution.py:12
  438.3 0.0 copy-done.3
  438.3 1.1 fusion.3
  439.4 108.4 %reduce-scatter.5.cloned.1.call-done = f32[32,8192]{1,0:T(8,128)} async-done(((f32[512,8192]{1,0:T(8,128)}), f32[32,8192]{1,0:T(8,128)}) %reduce-scatter.5.cloned.1.call-update) | async-done | bytes 1048592 | tf_op jit(solution)/shard_map/reduce_scatter | solution.py:27
  547.8 2.3 fusion.1
  (3 shorter events, 0.0 us)
Async XLA Ops:
  7.2 1.0 copy-start
  7.2 84.1 %reduce-scatter.7.cloned.1.call-start = ((), (), s32[]{:S(2)}) async-start(), calls=%async_computation.5 | async-start | bytes 278528
  9.9 340.1 %all-reduce.2.cloned.1.call-start = ((), (), s32[]{:S(2)}) async-start(), calls=%async_computation.4 | async-start | bytes 1048576 | tf_op jit(solution)/shard_map/psum | solution.py:49
  94.2 334.6 %all-gather.3.cloned.1.call-start = ((), (), s32[]{:S(2)}) async-start(), calls=%async_computation.3 | async-start | bytes 8912896 | tf_op jit(solution)/shard_map/all_gather | solution.py:37
  94.9 452.9 %reduce-scatter.5.cloned.1.call-start = ((), (), s32[]{:S(2)}) async-start(), calls=%async_computation.2 | async-start | bytes 17825792 | tf_op jit(solution)/shard_map/reduce_scatter | solution.py:27
  106.4 1.0 copy-start.1
  106.4 1.1 copy-start.2
  351.9 86.3 %copy-start.3 = (bf16[512,16]{0,1:T(8,128)(2,1)S(1)}, bf16[512,16]{0,1:T(8,128)(2,1)}, u32[]{:S(2)}) copy-start(bf16[512,16]{0,1:T(8,128)(2,1)} %param.7) | copy-start | bytes 49156
Sparse Core Ops, SparseCore 0:
  12.0 79.2 reduce-scatter.6
  98.2 251.8 all-reduce.1
  352.8 75.9 all-gather.2
  432.8 114.9 reduce-scatter.4
where the time goes:
time: 557 us
  waiting for transfers between devices  440 us (79%)
  blocking collectives  68.4 us (12%)
  matrix products  28.6 us (5%)
  between operations  13.8 us (2%)
    psum x1, waiting for transfers between devices, per_device(): second_sum = lax.psum(second_part, ('dp', 'tensor'))  173 us
    reduce_scatter x1, waiting for transfers between devices, per_device(): lax.psum_scatter(partial_value, 'tensor', scatter_dimension=0, tiled=True)  108 us
    unnamed x5, waiting for transfers between devices  82.1 us
    all_gather x1, waiting for transfers between devices, per_device(): lax.all_gather(cotangent, 'tensor', axis=0, tiled=True)  76.8 us
    psum x1, blocking collectives, per_device(): first_sum = lax.psum(first_part, 'dp')  51 us
    all_gather x1, blocking collectives, per_device(): lax.all_gather(low_rows, 'tensor', axis=0, tiled=True)  17.4 us
    dot_general x1, matrix products, per_device(): partial_value = jnp.dot(tokens, weight, preferred_element_type=jnp.float32)  11.5 us
  transfers between devices with their start and end apart: 4, of which 4 were waited for; matrix products, arithmetic and copies ran while one was open for 5% of the time, Pallas kernels for 0%

commit v1 on v0

v1 whole, which is shorter than its diff:
```python
import functools
import math

import jax
import jax.numpy as jnp
from jax import lax
from jax.experimental import pallas as pl
from jax.experimental.pallas import tpu as pltpu
from jax.sharding import PartitionSpec as P

MESH = pl.DeviceIdType.MESH
F32, BF16 = jnp.float32, jnp.bfloat16
SCALE = 0.5
FACTOR = SCALE / math.sqrt(8192)
CHUNKS, CW = 4, 512
HOPS = ((4, 3), (3, 4))


def dot(a, b, da, db):
    return lax.dot_general(a, b, (((da,), (db,)), ((), ())), preferred_element_type=F32)


def kernel(tok, w, down, up, cot, out, tg, ga, gb,
           wg, tokg, cotg, upv, dnv, lx, ly, lowv, lgx, lgv, of, os, orx, ob, gf, gs, gr, tgv, gab, sibin, zin, gav,
           loc, wa_s, wa_r, wz_s, wz_r, ws_s, ws_r, c1_s, c1_r, c2_s, c2_r, t_s, t_r, lx_s, lx_r, ly_s, ly_r,
           lgx_s, lgx_r, lgy_s, lgy_r, o1_s, o1_r, o2_s, o2_r, g_s, g_r, sb_s, sb_r, z_s, z_r, gy_s, gy_r, gx_s, gx_r):
    dp, t = lax.axis_index("dp"), lax.axis_index("tensor")
    z, c = lax.div(dp, 2), lax.rem(dp, 2)
    y, x = lax.div(t, 4), lax.rem(t, 4)

    def row(d):
        return (dp, y * 4 + lax.rem(x + d, 4))

    def col(d):
        return (dp, lax.rem(y + d, 4) * 4 + x)

    def zed(d):
        return (lax.rem(z + d, 8) * 2 + c, t)

    sib = (z * 2 + 1 - c, t)
    sends = []

    def rc(src, dst, ss, rs, dev):
        return pltpu.make_async_remote_copy(src, dst, ss, rs, device_id=dev, device_id_type=MESH)

    def push(*a):
        cp = rc(*a)
        cp.start()
        sends.append(cp)
        return cp

    def local(src, dst, i):
        cp = pltpu.make_async_copy(src, dst, loc.at[i])
        cp.start()
        return cp

    def slab(i, size):
        return pl.ds(pl.multiple_of(i * size, size), size)

    ld_tok = local(tok, tokg.at[:, pl.ds(0, 512)], 0)
    ld_dn = local(down, dnv, 1)
    ld_up = local(up.at[:, slab(x, 2048)], upv, 2)
    ld_cot = local(cot.at[:, slab(x, 2048)], cotg.at[0, slab(x, 32), :], 3)
    ld_w = local(w.at[:, slab(x, 2048)], wg.at[0], 4)

    bar = pltpu.get_barrier_semaphore()
    peers = [row(d) for d in (1, 2, 3)] + [col(d) for d in (1, 2, 3)] + [zed(d) for d in range(1, 8)] + [sib]
    for dev in peers:
        pl.semaphore_signal(bar, inc=1, device_id=dev, device_id_type=MESH)
    pl.semaphore_wait(bar, len(peers))

    wa = [[None] * 4 for _ in range(CHUNKS)]
    c1 = [None] * 4

    def send_w(j):
        for d in (2, 1, 3):
            n0 = pl.multiple_of(lax.rem(x + d, 4) * 2048 + j * CW, CW)
            wa[j][d] = push(w.at[slab(dp, 32), pl.ds(n0, CW)],
                            wg.at[4 - d, slab(dp, 32), pl.ds(j * CW, CW)], wa_s.at[j, d], wa_r.at[j, d], row(d))

    send_w(0)
    for d in (2, 1, 3):
        c1[d] = push(cot.at[:, slab(lax.rem(x + d, 4), 2048)], cotg.at[0, slab(x, 32), :], c1_s.at[d], c1_r.at[d], row(d))
    for j in range(1, CHUNKS):
        send_w(j)

    ld_tok.wait()
    ld_dn.wait()
    lx[0] = dot(dnv[...], tokg[:, pl.ds(0, 512)], 1, 1)
    lxc = [None] + [push(lx.at[0], lx.at[4 - d], lx_s.at[d], lx_r.at[d], row(d)) for d in (1, 2, 3)]

    ld_cot.wait()
    for d in (1, 2, 3):
        rc(cotg.at[0, slab(x, 32), :], cotg.at[0, slab(lax.rem(x + 4 - d, 4), 32), :], c1_s.at[d], c1_r.at[d],
           row(d)).wait_recv()
    c2 = [None] + [push(cotg.at[0], cotg.at[4 - d], c2_s.at[d], c2_r.at[d], col(d)) for d in (1, 2, 3)]
    tc = [None] + [push(tok, tokg.at[:, pl.ds((4 - d) * 512, 512)], t_s.at[d], t_r.at[d], row(d)) for d in (1, 2, 3)]
    ld_up.wait()
    lgx[0] = dot(upv[...], cotg[0], 1, 1)
    lgxc = [None] + [push(lgx.at[0], lgx.at[4 - d], lgx_s.at[d], lgx_r.at[d], row(d)) for d in (1, 2, 3)]

    def part(zz, cc, j):
        return wg.at[pl.ds(1, 3), slab(zz * 2 + cc, 32), pl.ds(j * CW, CW)]

    def origin(up_, s):
        return lax.rem(z + (8 - s if up_ else s), 8)

    def to_sib(zz, j, i):
        push(part(zz, c, j), part(zz, c, j), ws_s.at[j, i], ws_r.at[j, i], sib)

    def send_z(zz, j, k, s):
        push(part(zz, c, j), part(zz, c, j), wz_s.at[k, j, s], wz_r.at[k, j, s], zed(1 if k == 0 else 7))

    def small_low():
        for d in (1, 2, 3):
            lxc[d].wait_recv()
        ly[0] = (lx[0] + lx[1]) + (lx[2] + lx[3])
        return [None] + [push(ly.at[0], ly.at[4 - d], ly_s.at[d], ly_r.at[d], col(d)) for d in (1, 2, 3)]

    def small_lg():
        for d in (1, 2, 3):
            lgxc[d].wait_recv()
        lgv[0] = ((lgx[0] + lgx[1]) + (lgx[2] + lgx[3])).astype(BF16)
        return [None] + [push(lgv.at[0], lgv.at[4 - d], lgy_s.at[d], lgy_r.at[d], col(d)) for d in (1, 2, 3)]

    for pair in ((0, 1), (2, 3)):
        for j in pair:
            for d in (1, 2, 3):
                wa[j][d].wait_recv()
            send_z(z, j, 0, 1)
            send_z(z, j, 1, 1)
            to_sib(z, j, 0)
        if pair[0] == 0:
            lyc = small_low()
            lgyc = small_lg()
        for s in range(1, 5):
            for j in pair:
                for k in (0, 1):
                    if s > HOPS[j % 2][k]:
                        continue
                    zz = origin(k == 0, s)
                    rc(part(zz, c, j), part(zz, c, j), wz_s.at[k, j, s], wz_r.at[k, j, s], zed(1)).wait_recv()
                    if s < HOPS[j % 2][k]:
                        send_z(zz, j, k, s + 1)
                    to_sib(zz, j, s if k == 0 else 4 + s)

    def wait_sib(j):
        rc(part(z, c, j), part(z, 1 - c, j), ws_s.at[j, 0], ws_r.at[j, 0], sib).wait_recv()
        for k in (0, 1):
            for s in range(1, HOPS[j % 2][k] + 1):
                zz, i = origin(k == 0, s), (s if k == 0 else 4 + s)
                rc(part(zz, c, j), part(zz, 1 - c, j), ws_s.at[j, i], ws_r.at[j, i], sib).wait_recv()

    for d in (1, 2, 3):
        lyc[d].wait_recv()
        lgyc[d].wait_recv()
    lowv[...] = ((ly[0] + ly[1]) + (ly[2] + ly[3])).astype(BF16)

    ld_w.wait()
    for d in (1, 2, 3):
        tc[d].wait_recv()
    o1 = [[None] * 4 for _ in range(CHUNKS)]
    for j in range(CHUNKS):
        wait_sib(j)

        @pl.loop(0, 2)
        def _(q):
            cols = slab(j * 2 + q, 256)
            acc = dot(tokg[...], wg[:, :, cols].reshape(2048, 256), 1, 0)
            of[:, cols] = acc
            os[:, cols] = acc.astype(BF16)

        for d in (2, 1, 3):
            o1[j][d] = push(os.at[slab(lax.rem(y + d, 4), 128), pl.ds(j * CW, CW)], orx.at[3 - d, :, pl.ds(j * CW, CW)],
                            o1_s.at[j, d], o1_r.at[j, d], col(d))

    for d in (1, 2, 3):
        c2[d].wait_recv()
    gc = [[None] * 2 for _ in range(4)]
    for r in (2, 1, 3):
        for h in range(2):
            acc = dot(cotg[...].reshape(512, 2048), wg[r, pl.ds(h * 256, 256), :], 1, 1)
            gs[r - 1, :, pl.ds(h * 256, 256)] = acc.astype(BF16)
            gc[r][h] = push(gs.at[r - 1, :, pl.ds(h * 256, 256)], gr.at[3 - r, :, pl.ds(h * 256, 256)],
                            g_s.at[r, h], g_r.at[r, h], row(r))

    parts_a = [dot(lgv[r], tokg[slab(lax.rem(y + r, 4), 128), pl.ds(0, 512)], 1, 0) for r in range(4)]
    gab[0] = (parts_a[0] + parts_a[1]) + (parts_a[2] + parts_a[3])
    parts_b = [dot(lowv[:, slab(lax.rem(y + r, 4), 128)], cotg[r, :, slab(y, 512)], 1, 0) for r in range(4)]
    gab[1] = (parts_b[0] + parts_b[1]) + (parts_b[2] + parts_b[3])
    sb0 = push(gab.at[1 - c], sibin, sb_s.at[0], sb_r.at[0], sib)

    for h in range(2):
        gf[:, pl.ds(h * 256, 256)] = dot(cotg[...].reshape(512, 2048), wg[0, pl.ds(h * 256, 256), :], 1, 1)

    sb0.wait_recv()
    zin[z] = gab[c] + sibin[...]
    zc = [None] + [push(zin.at[z], zin.at[z], z_s.at[d], z_r.at[d], zed(d)) for d in range(1, 8)]

    o2 = [[None] * 4 for _ in range(CHUNKS)]
    own = []
    for j in range(CHUNKS):
        cols = pl.ds(j * CW, CW)
        for d in (1, 2, 3):
            o1[j][d].wait_recv()
        acc = of[slab(y, 128), cols] + orx[0, :, cols].astype(F32) + orx[1, :, cols].astype(F32) + orx[2, :, cols].astype(F32)
        acc += SCALE * dot(lowv[:, slab(y, 128)], upv[:, cols], 0, 0)
        ob[:, cols] = acc.astype(BF16)
        here = pl.ds(pl.multiple_of(x * 2048 + j * CW, CW), CW)
        for d in (2, 1, 3):
            o2[j][d] = push(ob.at[slab(lax.rem(x + d, 4), 32), cols], out.at[:, here], o2_s.at[j, d], o2_r.at[j, d], row(d))
        own.append(local(ob.at[slab(x, 32), cols], out.at[:, here], 5 + j))

    for d in range(1, 8):
        rc(zin.at[z], zin.at[lax.rem(z + 8 - d, 8)], z_s.at[d], z_r.at[d], zed(d)).wait_recv()
    total = zin[0]
    for i in range(1, 8):
        total = total + zin[i]
    gab_t = gav
    gab_t[c] = total * FACTOR
    sb1 = push(gab_t.at[c], gab_t.at[c], sb_s.at[1], sb_r.at[1], sib)
    rc(gab_t.at[c], gab_t.at[1 - c], sb_s.at[1], sb_r.at[1], sib).wait_recv()
    half = slab(c, 8)
    mine = pl.ds(pl.multiple_of(x * 2048 + y * 512, 512), 512)
    gyc = [push(gab_t.at[1, half, :], gb.at[half, mine], gy_s.at[d], gy_r.at[d], col(d)) for d in (1, 2, 3)]
    gb_own = local(gab_t.at[1, half, :], gb.at[half, mine], 9)

    for h in range(2):
        cols = pl.ds(h * 256, 256)
        for r in (1, 2, 3):
            gc[r][h].wait_recv()
        for q in range(4):
            rows = pl.ds(q * 128, 128)
            acc = gf[rows, cols] + gr[0, rows, cols].astype(F32) + gr[1, rows, cols].astype(F32) + gr[2, rows, cols].astype(F32)
            acc += SCALE * dot(lgv[q], dnv[:, cols], 0, 0)
            tgv[slab(lax.rem(y + q, 4), 128), cols] = acc.astype(BF16)
    tg_out = local(tgv, tg, 10)

    gb_own.wait()
    for d, cp in zip((1, 2, 3), gyc):
        there = pl.ds(pl.multiple_of(x * 2048 + lax.rem(y + 4 - d, 4) * 512, 512), 512)
        rc(gab_t.at[1, half, :], gb.at[half, there], gy_s.at[d], gy_r.at[d], col(d)).wait_recv()
    quarter = slab(x, 2048)
    for d in (1, 2, 3):
        push(gb.at[half, quarter], gb.at[half, quarter], gx_s.at[d], gx_r.at[d], row(d))
    for d in (1, 2, 3):
        there = slab(lax.rem(x + 4 - d, 4), 2048)
        rc(gb.at[half, quarter], gb.at[half, there], gx_s.at[d], gx_r.at[d], row(d)).wait_recv()
    push(gb.at[half, :], gb.at[half, :], sb_s.at[2], sb_r.at[2], sib)
    ga_out = local(gab_t.at[0], ga, 11)
    rc(gb.at[half, :], gb.at[slab(1 - c, 8), :], sb_s.at[2], sb_r.at[2], sib).wait_recv()

    for j in range(CHUNKS):
        own[j].wait()
        for d in (1, 2, 3):
            there = pl.ds(pl.multiple_of(lax.rem(x + 4 - d, 4) * 2048 + j * CW, CW), CW)
            rc(ob.at[slab(0, 32), pl.ds(j * CW, CW)], out.at[:, there], o2_s.at[j, d], o2_r.at[j, d], row(d)).wait_recv()
    tg_out.wait()
    ga_out.wait()
    for cp in sends:
        cp.wait_send()


def per_device(tokens, weight, down_adapter, up_adapter, cotangent):
    dma = pltpu.SemaphoreType.DMA
    any_ = pl.BlockSpec(memory_space=pl.ANY)
    sems = [(12,)] + [(CHUNKS, 4)] * 2 + [(2, CHUNKS, 5)] * 2 + [(CHUNKS, 9)] * 2 + [(4,)] * 14
    sems += [(CHUNKS, 4)] * 4 + [(4, 2)] * 2 + [(3,)] * 2 + [(8,)] * 2 + [(4,)] * 4
    out, token_gradient, grad_a, grad_b = pl.pallas_call(
        kernel,
        out_shape=(
            jax.ShapeDtypeStruct((32, 8192), BF16),
            jax.ShapeDtypeStruct((512, 512), BF16),
            jax.ShapeDtypeStruct((16, 512), F32),
            jax.ShapeDtypeStruct((16, 8192), F32),
        ),
        in_specs=[any_] * 5,
        out_specs=(any_,) * 4,
        scratch_shapes=[
            pltpu.VMEM((4, 512, 2048), BF16),
            pltpu.VMEM((512, 2048), BF16),
            pltpu.VMEM((4, 128, 2048), BF16),
            pltpu.VMEM((16, 2048), BF16),
            pltpu.VMEM((16, 512), BF16),
            pltpu.VMEM((4, 16, 512), F32),
            pltpu.VMEM((4, 16, 512), F32),
            pltpu.VMEM((16, 512), BF16),
            pltpu.VMEM((4, 16, 128), F32),
            pltpu.VMEM((4, 16, 128), BF16),
            pltpu.VMEM((512, 2048), F32),
            pltpu.VMEM((512, 2048), BF16),
            pltpu.VMEM((3, 128, 2048), BF16),
            pltpu.VMEM((128, 2048), BF16),
            pltpu.VMEM((512, 512), F32),
            pltpu.VMEM((3, 512, 512), BF16),
            pltpu.VMEM((3, 512, 512), BF16),
            pltpu.VMEM((512, 512), BF16),
            pltpu.VMEM((2, 16, 512), F32),
            pltpu.VMEM((16, 512), F32),
            pltpu.VMEM((8, 16, 512), F32),
            pltpu.VMEM((2, 16, 512), F32),
        ] + [dma(s) for s in sems],
        compiler_params=pltpu.CompilerParams(
            collective_id=0, has_side_effects=True, vmem_limit_bytes=56 * 2**20
        ),
        name="projection",
    )(tokens, weight, down_adapter.T, up_adapter, cotangent)
    return out, token_gradient, grad_a.T, grad_b


def solution(mesh):
    placed = (
        P("dp", "tensor"),
        P("tensor", None),
        P("tensor", None),
        P(),
        P(("dp", "tensor"), None),
    )
    return jax.shard_map(
        per_device,
        mesh=mesh,
        in_specs=placed,
        out_specs=(P(("dp", "tensor"), None), P("dp", "tensor"), P("tensor", None), P()),
        check_vma=False,
    )
```

time: 557 us -> 133 us (0.24)
  waiting for transfers between devices: 440 us -> 0 us
  Pallas kernels: 0 us -> 125 us
  blocking collectives: 68.4 us -> 0 us
  matrix products: 28.6 us -> 0 us
  between operations: 13.8 us -> 0.64 us
    psum x1 -> x0, waiting for transfers between devices: 173 us -> none  [per_device(): second_sum = lax.psum(second_part, ('dp', 'tensor'))]
    pallas_call x0 -> x1, Pallas kernels: none -> 125 us  [per_device(): pl.pallas_call(kernel, out_shape=(jax.ShapeDtypeStruct((32, 8192), BF16),...]
    reduce_scatter x1 -> x0, waiting for transfers between devices: 108 us -> none  [per_device(): lax.psum_scatter(partial_value, 'tensor', scatter_dimension=0, tiled=True)]
    unnamed x5 -> x0, waiting for transfers between devices: 82.1 us -> none
    all_gather x1 -> x0, waiting for transfers between devices: 76.8 us -> none  [per_device(): lax.all_gather(cotangent, 'tensor', axis=0, tiled=True)]
    psum x1 -> x0, blocking collectives: 51 us -> none  [per_device(): first_sum = lax.psum(first_part, 'dp')]
    dot_general x7 -> x0, matrix products: 26.9 us -> none  [the longest x1 11.5 us: per_device(): partial_value = jnp.dot(tokens, weight, preferred_element_type=jnp.float32)]
    all_gather x1 -> x0, blocking collectives: 17.4 us -> none  [per_device(): lax.all_gather(low_rows, 'tensor', axis=0, tiled=True)]
  transfers between devices with their start and end apart: 4 -> 0, of which waited for: 4 -> 0; matrix products, arithmetic and copies ran while one was open for 5% -> 0% of each run, Pallas kernels for 0% -> 0%
where the time goes in v1:
time: 133 us
  Pallas kernels  125 us (94%)
  local copies, waits for them, and re-layouts  6.98 us (5%)
    pallas_call x1, Pallas kernels, per_device(): pl.pallas_call(kernel, out_shape=(jax.ShapeDtypeStruct((32, 8192), BF16),...  125 us
    unnamed x4, local copies, waits for them, and re-layouts  6.98 us

profile of v1, /device:TPU:1, one launch (start us, length us, event | category | flops | bytes accessed | tf_op | source)
XLA Modules:
  0.0 133.0 jit_solution(3287969505272978307)
XLA Ops:
  0.6 125.4 %projection.1 = (bf16[32,8192]{1,0:T(8,128)(2,1)}, bf16[512,512]{1,0:T(8,128)(2,1)}, f32[16,512]{1,0:T(8,128)}, f32[16,8192]{1,0:T(8,128)}) custom-call(bf16[512,512]{1,0:T(8,128)(2,1)} %tok.1, bf16[512,8192]{1,0:T(8,128)(2,1)} %w.1, bf16[16,512]{1,0:T(8,128)(2,1)} %bitcast.3, bf16[16,8192]{1,0:T(8,128)(2,1)} %up.1, bf16[32,8192]{1,0:T(8,128)(2,1)} %cot.1), custom_call_target="tpu_custom_call" | custom-call | tf_op jit(solution)/shard_map/projection/pallas_call | solution.py:269
  126.0 1.9 %copy.13 = bf16[32,8192]{1,0:T(8,128)(2,1)} copy(bf16[32,8192]{1,0:T(8,128)(2,1)} %get-tuple-element.16) | data formatting | bytes 1048576
  127.9 1.9 %copy.14 = bf16[512,512]{1,0:T(8,128)(2,1)} copy(bf16[512,512]{1,0:T(8,128)(2,1)} %get-tuple-element.17) | data formatting | bytes 1048576
  129.7 1.4 %copy.15 = f32[512,16]{0,1:T(8,128)} copy(f32[512,16]{0,1:T(8,128)} %bitcast.2) | data formatting | bytes 65536
  131.1 1.9 %copy.16 = f32[16,8192]{1,0:T(8,128)} copy(f32[16,8192]{1,0:T(8,128)} %get-tuple-element.19) | data formatting | bytes 1048576

commit v2 on v0

v2 whole, which is shorter than its diff:
```python
import math

import jax
import jax.numpy as jnp
from jax import lax
from jax.experimental import pallas as pl
from jax.experimental.pallas import tpu as pltpu
from jax.sharding import PartitionSpec as P

MESH = pl.DeviceIdType.MESH
F32, BF16 = jnp.float32, jnp.bfloat16
SCALE = 0.5
FACTOR = SCALE / math.sqrt(8192)
CHUNKS, CW = 4, 512
HOPS = ((4, 3), (3, 4))

TRANSFERS = dict(wa=(CHUNKS, 4), wz=(2, CHUNKS, 5), ws=(CHUNKS, 9), c1=(4,), c2=(3, 2), t=(3, 2), lx=(4,), ly=(4,), lgx=(4,),
                 lgy=(4,), om=(CHUNKS, 2), o1=(CHUNKS, 2, 2), o2=(CHUNKS, 4), gm=(2,), g=(2, 2), sb=(3,), z=(8,), gy=(4,), gx=(4,))
BUFFERS = dict(
    wg=((4, 512, 2048), BF16),
    tokg=((512, 2048), BF16),
    cotg=((4, 128, 2048), BF16),
    upv=((16, 2048), BF16), dnv=((16, 512), BF16),
    lx=((4, 16, 512), F32), ly=((4, 16, 512), F32), lowv=((16, 512), BF16),
    lgx=((4, 16, 128), F32), lgv=((4, 16, 128), BF16),
    of=((512, 2048), F32), os=((512, 2048), BF16), om=((2, 128, 1024), BF16), orx=((2, 128, 2048), BF16), ob=((128, 2048), BF16),
    gf=((512, 512), F32), gs=((3, 512, 512), BF16), gt=((2, 512, 256), F32), gm=((2, 512, 256), BF16), gr=((2, 512, 512), BF16), tgv=((512, 512), BF16),
    gab=((2, 16, 512), F32), sibin=((16, 512), F32), zin=((8, 16, 512), F32), gav=((2, 16, 512), F32),
)


def dot(a, b, da, db):
    return lax.dot_general(a, b, (((da,), (db,)), ((), ())), preferred_element_type=F32)


def kernel(tok, w, down, up, cot, out, tg, ga, gb, *scratch):
    (wg, tokg, cotg, upv, dnv, lx, ly, lowv, lgx, lgv, of, os, om, orx, ob, gf, gs, gt, gm, gr, tgv, gab, sibin, zin, gav) = scratch[: len(BUFFERS)]
    loc, sems = scratch[len(BUFFERS)], scratch[len(BUFFERS) + 1 :]
    sems = {name: sems[2 * i : 2 * i + 2] for i, name in enumerate(TRANSFERS)}
    dp, t = lax.axis_index("dp"), lax.axis_index("tensor")
    z, c = lax.div(dp, 2), lax.rem(dp, 2)
    y, x = lax.div(t, 4), lax.rem(t, 4)

    def row(d):
        return (dp, y * 4 + lax.rem(x + d, 4))

    def col(d):
        return (dp, lax.rem(y + d, 4) * 4 + x)

    def zed(d):
        return (lax.rem(z + d, 8) * 2 + c, t)

    sib = (z * 2 + 1 - c, t)
    sends, pending, locals_ = [], {}, []

    def remote(name, idx, src, dst, dev):
        send, recv = sems[name]
        return pltpu.make_async_remote_copy(src, dst, send.at[idx], recv.at[idx], device_id=dev, device_id_type=MESH)

    def push(name, idx, src, dst, dev):
        cp = remote(name, idx, src, dst, dev)
        cp.start()
        sends.append(cp)
        pending[name, idx] = cp

    def arrive(name, idx, dst=None):
        cp = pending.pop((name, idx))
        (cp if dst is None else remote(name, idx, dst, dst, sib)).wait_recv()

    def local(src, dst):
        cp = pltpu.make_async_copy(src, dst, loc.at[len(locals_)])
        cp.start()
        locals_.append(cp)
        return cp

    def slab(i, size):
        return pl.ds(pl.multiple_of(i * size, size), size)

    ld_w = local(w.at[:, slab(x, 2048)], wg.at[0])
    ld_tok = local(tok, tokg.at[:, pl.ds(0, 512)])
    ld_dn = local(down, dnv)
    ld_up = local(up.at[:, slab(x, 2048)], upv)
    ld_cot = local(cot.at[:, slab(x, 2048)], cotg.at[0, slab(x, 32), :])

    bar = pltpu.get_barrier_semaphore()
    peers = [row(d) for d in (1, 2, 3)] + [col(d) for d in (1, 2, 3)] + [zed(d) for d in range(1, 8)] + [sib]
    for dev in peers:
        pl.semaphore_signal(bar, inc=1, device_id=dev, device_id_type=MESH)
    pl.semaphore_wait(bar, len(peers))

    for j in range(CHUNKS):
        for d in (2, 1, 3):
            n0 = pl.multiple_of(lax.rem(x + d, 4) * 2048 + j * CW, CW)
            push("wa", (j, d), w.at[slab(dp, 32), pl.ds(n0, CW)], wg.at[4 - d, slab(dp, 32), pl.ds(j * CW, CW)], row(d))
    for d in (2, 1, 3):
        push("c1", (d,), cot.at[:, slab(lax.rem(x + d, 4), 2048)], cotg.at[0, slab(x, 32), :], row(d))

    ld_tok.wait()
    ld_dn.wait()
    lx[0] = dot(dnv[...], tokg[:, pl.ds(0, 512)], 1, 1)
    for d in (1, 2, 3):
        push("lx", (d,), lx.at[0], lx.at[4 - d], row(d))

    def half(ref, r, h):
        return ref.at[r, pl.ds(h * 64, 64), :] if ref is cotg else ref.at[pl.ds(h * 256, 256), pl.ds(r * 512, 512)]

    def spread(name, ref, to):
        for i in (0, 1):
            push(name, (0, i), half(ref, 0, i), half(ref, 3, i), to(1))
            push(name, (1, i), half(ref, 0, 1 - i), half(ref, 1, 1 - i), to(3))

    def spread_on(name, ref, to):
        arrive(name, (0, 0))
        push(name, (2, 0), half(ref, 3, 0), half(ref, 2, 0), to(1))
        arrive(name, (1, 0))
        push(name, (2, 1), half(ref, 1, 1), half(ref, 2, 1), to(3))

    def spread_end(name):
        for idx in ((0, 1), (1, 1), (2, 0), (2, 1)):
            arrive(name, idx)

    spread("t", tokg, row)

    def part(zz, cc, j):
        return wg.at[pl.ds(1, 3), slab(zz * 2 + cc, 32), pl.ds(j * CW, CW)]

    def origin(k, s):
        return lax.rem(z + (8 - s if k == 0 else s), 8)

    def to_sib(zz, j, i):
        push("ws", (j, i), part(zz, c, j), part(zz, c, j), sib)

    def send_z(zz, j, k, s):
        push("wz", (k, j, s), part(zz, c, j), part(zz, c, j), zed(1 if k == 0 else 7))

    def step_z(s, j):
        for k in (0, 1):
            if s <= HOPS[j % 2][k]:
                zz = origin(k, s)
                arrive("wz", (k, j, s), part(zz, c, j))
                if s < HOPS[j % 2][k]:
                    send_z(zz, j, k, s + 1)
                to_sib(zz, j, s if k == 0 else 4 + s)

    for j in range(CHUNKS):
        for d in (1, 2, 3):
            arrive("wa", (j, d))
        send_z(z, j, 0, 1)
        send_z(z, j, 1, 1)
        to_sib(z, j, 0)
    step_z(1, 0)
    step_z(1, 1)

    ld_up.wait()
    ld_cot.wait()
    for d in (1, 2, 3):
        arrive("c1", (d,), cotg.at[0, slab(lax.rem(x + 4 - d, 4), 32), :])
    lgx[0] = dot(upv[...], cotg[0], 1, 1)
    for d in (1, 2, 3):
        push("lgx", (d,), lgx.at[0], lgx.at[4 - d], row(d))
    for d in (1, 2, 3):
        arrive("lx", (d,))
    ly[0] = (lx[0] + lx[1]) + (lx[2] + lx[3])
    for d in (1, 2, 3):
        push("ly", (d,), ly.at[0], ly.at[4 - d], col(d))
    spread("c2", cotg, col)
    step_z(1, 2)
    step_z(1, 3)
    for j in range(CHUNKS):
        step_z(2, j)
    spread_on("t", tokg, row)
    spread_on("c2", cotg, col)
    for d in (1, 2, 3):
        arrive("lgx", (d,))
    lgv[0] = ((lgx[0] + lgx[1]) + (lgx[2] + lgx[3])).astype(BF16)
    for d in (1, 2, 3):
        push("lgy", (d,), lgv.at[0], lgv.at[4 - d], col(d))
    for j in range(CHUNKS):
        step_z(3, j)

    for d in (1, 2, 3):
        arrive("ly", (d,))
        arrive("lgy", (d,))
    lowv[...] = ((ly[0] + ly[1]) + (ly[2] + ly[3])).astype(BF16)
    spread_end("c2")
    parts_a = [dot(lgv[r], tokg[slab(lax.rem(y + r, 4), 128), pl.ds(0, 512)], 1, 0) for r in range(4)]
    gab[0] = (parts_a[0] + parts_a[1]) + (parts_a[2] + parts_a[3])
    parts_b = [dot(lowv[:, slab(lax.rem(y + r, 4), 128)], cotg[r, :, slab(y, 512)], 1, 0) for r in range(4)]
    gab[1] = (parts_b[0] + parts_b[1]) + (parts_b[2] + parts_b[3])
    push("sb", (0,), gab.at[1 - c], sibin, sib)

    for j in range(CHUNKS):
        step_z(4, j)

    def weight(j):
        arrive("ws", (j, 0), part(z, 1 - c, j))
        for k in (0, 1):
            for s in range(1, HOPS[j % 2][k] + 1):
                arrive("ws", (j, s if k == 0 else 4 + s), part(origin(k, s), 1 - c, j))

    up1, up2, up3 = (slab(lax.rem(y + d, 4), 128) for d in (1, 2, 3))

    def forward(j):
        @pl.loop(0, 2)
        def _(q):
            cols = slab(j * 2 + q, 256)
            acc = dot(tokg[...], wg[:, :, cols].reshape(2048, 256), 1, 0)
            of[:, cols] = acc
            os[:, cols] = acc.astype(BF16)

        lo, hi, mid = pl.ds(j * CW, 256), pl.ds(j * CW + 256, 256), pl.ds(j * 256, 256)
        push("om", (j, 0), os.at[up2, lo], om.at[0, :, mid], col(1))
        push("om", (j, 1), os.at[up2, hi], om.at[1, :, mid], col(3))
        push("o1", (j, 0, 1), os.at[up1, hi], orx.at[0, :, hi], col(1))
        push("o1", (j, 1, 0), os.at[up3, lo], orx.at[1, :, lo], col(3))

    def forward_on(j):
        lo, hi, mid = pl.ds(j * CW, 256), pl.ds(j * CW + 256, 256), pl.ds(j * 256, 256)
        arrive("om", (j, 0))
        os[up1, lo] = (of[up1, lo] + om[0, :, mid].astype(F32)).astype(BF16)
        push("o1", (j, 0, 0), os.at[up1, lo], orx.at[0, :, lo], col(1))
        arrive("om", (j, 1))
        os[up3, hi] = (of[up3, hi] + om[1, :, mid].astype(F32)).astype(BF16)
        push("o1", (j, 1, 1), os.at[up3, hi], orx.at[1, :, hi], col(3))

    def backward(r):
        for h in (1, 0) if r == 1 else (0, 1):
            cols = pl.ds(h * 256, 256)
            acc = dot(cotg[...].reshape(512, 2048), wg[r, cols, :], 1, 1)
            if r == 0:
                gf[:, cols] = acc
            elif r == 2:
                gs[1, :, cols] = acc.astype(BF16)
                push("gm", (h,), gs.at[1, :, cols], gm.at[h], row(1 if h == 0 else 3))
            elif (r, h) in ((1, 0), (3, 1)):
                gt[h] = acc
            else:
                gs[r - 1, :, cols] = acc.astype(BF16)
                push("g", (1 - h, h), gs.at[r - 1, :, cols], gr.at[1 - h, :, cols], row(r))

    def backward_on(h):
        cols = pl.ds(h * 256, 256)
        arrive("gm", (h,))
        gs[2 * h, :, cols] = (gt[h] + gm[h].astype(F32)).astype(BF16)
        push("g", (h, h), gs.at[2 * h, :, cols], gr.at[h, :, cols], row(1 if h == 0 else 3))

    eight = slab(c, 8)

    def block(yy):
        return gb.at[eight, pl.ds(pl.multiple_of(x * 2048 + yy * 512, 512), 512)]

    arrive("sb", (0,))
    zin[z] = gab[c] + sibin[...]
    for d in range(1, 8):
        push("z", (d,), zin.at[z], zin.at[z], zed(d))
    ld_w.wait()
    for j in range(CHUNKS):
        weight(j)
    backward(2)
    spread_end("t")
    forward(0)
    backward(1)
    backward(3)
    forward(1)
    backward_on(0)
    backward_on(1)
    forward_on(0)
    for d in range(1, 8):
        arrive("z", (d,), zin.at[lax.rem(z + 8 - d, 8)])
    total = zin[0]
    for i in range(1, 8):
        total = total + zin[i]
    gav[c] = total * FACTOR
    push("sb", (1,), gav.at[c], gav.at[c], sib)
    forward(2)
    arrive("sb", (1,), gav.at[1 - c])
    ga_out = local(gav.at[0], ga)
    for d in (1, 2, 3):
        push("gy", (d,), gav.at[1, eight, :], block(y), col(d))
    gb_own = local(gav.at[1, eight, :], block(y))
    forward_on(1)
    forward(3)
    forward_on(2)
    backward(0)
    forward_on(3)

    def output(j):
        cols = pl.ds(j * CW, CW)
        for k in (0, 1):
            for h in (0, 1):
                arrive("o1", (j, k, h))
        acc = of[slab(y, 128), cols] + orx[0, :, cols].astype(F32) + orx[1, :, cols].astype(F32)
        acc += SCALE * dot(lowv[:, slab(y, 128)], upv[:, cols], 0, 0)
        ob[:, cols] = acc.astype(BF16)
        here = pl.ds(pl.multiple_of(x * 2048 + j * CW, CW), CW)
        for d in (2, 1, 3):
            push("o2", (j, d), ob.at[slab(lax.rem(x + d, 4), 32), cols], out.at[:, here], row(d))
        return local(ob.at[slab(x, 32), cols], out.at[:, here])

    gb_own.wait()
    for d in (1, 2, 3):
        arrive("gy", (d,), block(lax.rem(y + 4 - d, 4)))
    for d in (1, 2, 3):
        push("gx", (d,), gb.at[eight, slab(x, 2048)], gb.at[eight, slab(x, 2048)], row(d))
    own = [output(0), output(1), output(2)]
    for d in (1, 2, 3):
        arrive("gx", (d,), gb.at[eight, slab(lax.rem(x + 4 - d, 4), 2048)])
    push("sb", (2,), gb.at[eight, :], gb.at[eight, :], sib)
    own.append(output(3))

    for h in range(2):
        cols = pl.ds(h * 256, 256)
        arrive("g", (0, h))
        arrive("g", (1, h))
        for q in range(4):
            rows = pl.ds(q * 128, 128)
            acc = gf[rows, cols] + gr[0, rows, cols].astype(F32) + gr[1, rows, cols].astype(F32)
            acc += SCALE * dot(lgv[q], dnv[:, cols], 0, 0)
            tgv[slab(lax.rem(y + q, 4), 128), cols] = acc.astype(BF16)
    tg_out = local(tgv, tg)

    arrive("sb", (2,), gb.at[slab(1 - c, 8), :])
    for j in range(CHUNKS):
        own[j].wait()
        for d in (1, 2, 3):
            there = pl.ds(pl.multiple_of(lax.rem(x + 4 - d, 4) * 2048 + j * CW, CW), CW)
            arrive("o2", (j, d), out.at[:, there])
    tg_out.wait()
    ga_out.wait()
    for cp in sends:
        cp.wait_send()


def finish(a, b, c, d, oa, ob, oc, od, va, vb, vc, vd, sem):
    loads = [pltpu.make_async_copy(s, v, sem.at[0, i]) for i, (s, v) in enumerate(((a, va), (b, vb), (c, vc), (d, vd)))]
    stores = [pltpu.make_async_copy(v, o, sem.at[1, i]) for i, (v, o) in enumerate(((va, oa), (vb, ob), (vc, oc), (vd, od)))]
    for cp in loads:
        cp.start()
    for load, store in zip(loads, stores):
        load.wait()
        store.start()
    for cp in stores:
        cp.wait()


def per_device(tokens, weight, down_adapter, up_adapter, cotangent):
    dma = pltpu.SemaphoreType.DMA
    any_ = pl.BlockSpec(memory_space=pl.ANY)
    results = (
        jax.ShapeDtypeStruct((32, 8192), BF16),
        jax.ShapeDtypeStruct((512, 512), BF16),
        jax.ShapeDtypeStruct((16, 512), F32),
        jax.ShapeDtypeStruct((16, 8192), F32),
    )
    made = pl.pallas_call(
        kernel,
        out_shape=results,
        in_specs=[any_] * 5,
        out_specs=(any_,) * 4,
        scratch_shapes=[pltpu.VMEM(*b) for b in BUFFERS.values()]
        + [dma((16,))]
        + [dma(shape) for shape in TRANSFERS.values() for _ in range(2)],
        compiler_params=pltpu.CompilerParams(collective_id=0, has_side_effects=True, vmem_limit_bytes=56 * 2**20),
        name="projection",
    )(tokens, weight, down_adapter.T, up_adapter, cotangent)
    output, token_gradient, grad_a, grad_b = pl.pallas_call(
        finish,
        out_shape=results,
        in_specs=[any_] * 4,
        out_specs=(any_,) * 4,
        scratch_shapes=[pltpu.VMEM(r.shape, r.dtype) for r in results] + [dma((2, 4))],
        name="results",
    )(*made)
    return output, token_gradient, grad_a.T, grad_b


def solution(mesh):
    placed = (
        P("dp", "tensor"),
        P("tensor", None),
        P("tensor", None),
        P(),
        P(("dp", "tensor"), None),
    )
    return jax.shard_map(
        per_device,
        mesh=mesh,
        in_specs=placed,
        out_specs=(P(("dp", "tensor"), None), P("dp", "tensor"), P("tensor", None), P()),
        check_vma=False,
    )
```

time: 557 us -> 87.7 us (0.16)
  waiting for transfers between devices: 440 us -> 0 us
  Pallas kernels: 0 us -> 86.9 us
  blocking collectives: 68.4 us -> 0 us
  matrix products: 28.6 us -> 0 us
  between operations: 13.8 us -> 0.64 us
    psum x1 -> x0, waiting for transfers between devices: 173 us -> none  [per_device(): second_sum = lax.psum(second_part, ('dp', 'tensor'))]
    reduce_scatter x1 -> x0, waiting for transfers between devices: 108 us -> none  [per_device(): lax.psum_scatter(partial_value, 'tensor', scatter_dimension=0, tiled=True)]
    pallas_call x0 -> x2, Pallas kernels: none -> 86.9 us  [the longest x1 84.7 us: per_device(): pl.pallas_call(kernel, out_shape=results, in_specs=[any_] * 5, out_specs=...]
    unnamed x5 -> x0, waiting for transfers between devices: 82.1 us -> none
    all_gather x1 -> x0, waiting for transfers between devices: 76.8 us -> none  [per_device(): lax.all_gather(cotangent, 'tensor', axis=0, tiled=True)]
    psum x1 -> x0, blocking collectives: 51 us -> none  [per_device(): first_sum = lax.psum(first_part, 'dp')]
    dot_general x7 -> x0, matrix products: 26.9 us -> none  [the longest x1 11.5 us: per_device(): partial_value = jnp.dot(tokens, weight, preferred_element_type=jnp.float32)]
    all_gather x1 -> x0, blocking collectives: 17.4 us -> none  [per_device(): lax.all_gather(low_rows, 'tensor', axis=0, tiled=True)]
  transfers between devices with their start and end apart: 4 -> 0, of which waited for: 4 -> 0; matrix products, arithmetic and copies ran while one was open for 5% -> 0% of each run, Pallas kernels for 0% -> 0%
where the time goes in v2:
time: 87.7 us; the launch traced here: 87.6 us
  Pallas kernels  86.9 us (99%)
    pallas_call x1, Pallas kernels, per_device(): pl.pallas_call(kernel, out_shape=results, in_specs=[any_] * 5, out_specs=...  84.7 us
    pallas_call x1, Pallas kernels, per_device(): pl.pallas_call(finish, out_shape=results, in_specs=[any_] * 4, out_specs=...  2.26 us

profile of v2, /device:TPU:1, one launch (start us, length us, event | category | flops | bytes accessed | tf_op | source)
XLA Modules:
  0.0 87.6 jit_solution(17316250223591282081)
XLA Ops:
  0.6 84.7 %projection.1 = (bf16[32,8192]{1,0:T(8,128)(2,1)}, bf16[512,512]{1,0:T(8,128)(2,1)}, f32[16,512]{1,0:T(8,128)}, f32[16,8192]{1,0:T(8,128)}) custom-call(bf16[512,512]{1,0:T(8,128)(2,1)} %tok.1, bf16[512,8192]{1,0:T(8,128)(2,1)} %w.1, bf16[16,512]{1,0:T(8,128)(2,1)} %bitcast.2, bf16[16,8192]{1,0:T(8,128)(2,1)} %up.1, bf16[32,8192]{1,0:T(8,128)(2,1)} %cot.1), custom_call_target="tpu_custom_call" | custom-call | tf_op jit(solution)/shard_map/projection/pallas_call | solution.py:355
  85.3 2.3 %results.1 = (bf16[32,8192]{1,0:T(8,128)(2,1)}, bf16[512,512]{1,0:T(8,128)(2,1)}, f32[16,512]{1,0:T(8,128)}, f32[16,8192]{1,0:T(8,128)}) custom-call(bf16[32,8192]{1,0:T(8,128)(2,1)} %get-tuple-element.12.a, bf16[512,512]{1,0:T(8,128)(2,1)} %get-tuple-element.13.b, f32[16,512]{1,0:T(8,128)} %get-tuple-element.14.c, f32[16,8192]{1,0:T(8,128)} %get-tuple-element.15.d), custom_call_target="tpu_custom_call" | custom-call | tf_op jit(solution)/shard_map/results/pallas_call | solution.py:366

commit v3 on v2

--- a/solution.py
+++ b/solution.py
@@ -12,9 +12,10 @@
 SCALE = 0.5
 FACTOR = SCALE / math.sqrt(8192)
 CHUNKS, CW = 4, 512
+UNITS = ((2, 0), (2, 1), (1, 0), (3, 0), (1, 1), (3, 1))
 HOPS = ((4, 3), (3, 4))
 
-TRANSFERS = dict(wa=(CHUNKS, 4), wz=(2, CHUNKS, 5), ws=(CHUNKS, 9), c1=(4,), c2=(3, 2), t=(3, 2), lx=(4,), ly=(4,), lgx=(4,),
+TRANSFERS = dict(wa=(6,), wz=(2, 6, 5), ws=(6, 9), c1=(4,), c2=(3, 2), t=(3, 2), lx=(4,), ly=(4,), lgx=(4,),
                  lgy=(4,), om=(CHUNKS, 2), o1=(CHUNKS, 2, 2), o2=(CHUNKS, 4), gm=(2,), g=(2, 2), sb=(3,), z=(8,), gy=(4,), gx=(4,))
 BUFFERS = dict(
     wg=((4, 512, 2048), BF16),
@@ -88,18 +89,53 @@
         pl.semaphore_signal(bar, inc=1, device_id=dev, device_id_type=MESH)
     pl.semaphore_wait(bar, len(peers))
 
-    for j in range(CHUNKS):
-        for d in (2, 1, 3):
-            n0 = pl.multiple_of(lax.rem(x + d, 4) * 2048 + j * CW, CW)
-            push("wa", (j, d), w.at[slab(dp, 32), pl.ds(n0, CW)], wg.at[4 - d, slab(dp, 32), pl.ds(j * CW, CW)], row(d))
+    def send_w(u):
+        r, h = UNITS[u]
+        n0 = pl.multiple_of(lax.rem(x + 4 - r, 4) * 2048 + h * 1024, 1024)
+        push("wa", (u,), w.at[slab(dp, 32), pl.ds(n0, 1024)], wg.at[r, slab(dp, 32), pl.ds(h * 1024, 1024)], row(4 - r))
+
+    send_w(0)
+    send_w(1)
     for d in (2, 1, 3):
         push("c1", (d,), cot.at[:, slab(lax.rem(x + d, 4), 2048)], cotg.at[0, slab(x, 32), :], row(d))
-
-    ld_tok.wait()
-    ld_dn.wait()
-    lx[0] = dot(dnv[...], tokg[:, pl.ds(0, 512)], 1, 1)
-    for d in (1, 2, 3):
-        push("lx", (d,), lx.at[0], lx.at[4 - d], row(d))
+    for u in range(2, 6):
+        send_w(u)
+
+    def part(zz, cc, u):
+        r, h = UNITS[u]
+        return wg.at[r, slab(zz * 2 + cc, 32), pl.ds(h * 1024, 1024)]
+
+    def origin(k, s):
+        return lax.rem(z + (8 - s if k == 0 else s), 8)
+
+    def to_sib(zz, u, i):
+        push("ws", (u, i), part(zz, c, u), part(zz, c, u), sib)
+
+    def send_z(zz, u, k, s):
+        push("wz", (k, u, s), part(zz, c, u), part(zz, c, u), zed(1 if k == 0 else 7))
+
+    def start_z(u):
+        arrive("wa", (u,))
+        send_z(z, u, 0, 1)
+        send_z(z, u, 1, 1)
+        to_sib(z, u, 0)
+
+    def step_z(s, u):
+        hops = HOPS[u % 2]
+        for k in (0, 1):
+            if s <= hops[k]:
+                zz = origin(k, s)
+                arrive("wz", (k, u, s), part(zz, c, u))
+                if s < hops[k]:
+                    send_z(zz, u, k, s + 1)
+                to_sib(zz, u, s if k == 0 else 4 + s)
+
+    def weight(*units):
+        for u in units:
+            arrive("ws", (u, 0), part(z, 1 - c, u))
+            for k in (0, 1):
+                for s in range(1, HOPS[u % 2][k] + 1):
+                    arrive("ws", (u, s if k == 0 else 4 + s), part(origin(k, s), 1 - c, u))
 
     def half(ref, r, h):
         return ref.at[r, pl.ds(h * 64, 64), :] if ref is cotg else ref.at[pl.ds(h * 256, 256), pl.ds(r * 512, 512)]
@@ -119,84 +155,54 @@
         for idx in ((0, 1), (1, 1), (2, 0), (2, 1)):
             arrive(name, idx)
 
-    spread("t", tokg, row)
-
-    def part(zz, cc, j):
-        return wg.at[pl.ds(1, 3), slab(zz * 2 + cc, 32), pl.ds(j * CW, CW)]
-
-    def origin(k, s):
-        return lax.rem(z + (8 - s if k == 0 else s), 8)
-
-    def to_sib(zz, j, i):
-        push("ws", (j, i), part(zz, c, j), part(zz, c, j), sib)
-
-    def send_z(zz, j, k, s):
-        push("wz", (k, j, s), part(zz, c, j), part(zz, c, j), zed(1 if k == 0 else 7))
-
-    def step_z(s, j):
-        for k in (0, 1):
-            if s <= HOPS[j % 2][k]:
-                zz = origin(k, s)
-                arrive("wz", (k, j, s), part(zz, c, j))
-                if s < HOPS[j % 2][k]:
-                    send_z(zz, j, k, s + 1)
-                to_sib(zz, j, s if k == 0 else 4 + s)
-
-    for j in range(CHUNKS):
-        for d in (1, 2, 3):
-            arrive("wa", (j, d))
-        send_z(z, j, 0, 1)
-        send_z(z, j, 1, 1)
-        to_sib(z, j, 0)
+    start_z(0)
+    start_z(1)
+    ld_tok.wait()
+    ld_dn.wait()
+    lx[0] = dot(dnv[...], tokg[:, pl.ds(0, 512)], 1, 1)
+    for d in (1, 2, 3):
+        push("lx", (d,), lx.at[0], lx.at[4 - d], row(d))
     step_z(1, 0)
     step_z(1, 1)
-
     ld_up.wait()
     ld_cot.wait()
     for d in (1, 2, 3):
         arrive("c1", (d,), cotg.at[0, slab(lax.rem(x + 4 - d, 4), 32), :])
+    spread("c2", cotg, col)
     lgx[0] = dot(upv[...], cotg[0], 1, 1)
     for d in (1, 2, 3):
         push("lgx", (d,), lgx.at[0], lgx.at[4 - d], row(d))
+    spread("t", tokg, row)
+    start_z(2)
+    start_z(3)
+    step_z(2, 0)
+    step_z(2, 1)
+    start_z(4)
+    start_z(5)
     for d in (1, 2, 3):
         arrive("lx", (d,))
     ly[0] = (lx[0] + lx[1]) + (lx[2] + lx[3])
     for d in (1, 2, 3):
         push("ly", (d,), ly.at[0], ly.at[4 - d], col(d))
-    spread("c2", cotg, col)
     step_z(1, 2)
     step_z(1, 3)
-    for j in range(CHUNKS):
-        step_z(2, j)
+    step_z(3, 0)
+    step_z(3, 1)
+    step_z(1, 4)
+    step_z(1, 5)
+    spread_on("c2", cotg, col)
     spread_on("t", tokg, row)
-    spread_on("c2", cotg, col)
     for d in (1, 2, 3):
         arrive("lgx", (d,))
     lgv[0] = ((lgx[0] + lgx[1]) + (lgx[2] + lgx[3])).astype(BF16)
     for d in (1, 2, 3):
         push("lgy", (d,), lgv.at[0], lgv.at[4 - d], col(d))
-    for j in range(CHUNKS):
-        step_z(3, j)
-
-    for d in (1, 2, 3):
-        arrive("ly", (d,))
-        arrive("lgy", (d,))
-    lowv[...] = ((ly[0] + ly[1]) + (ly[2] + ly[3])).astype(BF16)
-    spread_end("c2")
-    parts_a = [dot(lgv[r], tokg[slab(lax.rem(y + r, 4), 128), pl.ds(0, 512)], 1, 0) for r in range(4)]
-    gab[0] = (parts_a[0] + parts_a[1]) + (parts_a[2] + parts_a[3])
-    parts_b = [dot(lowv[:, slab(lax.rem(y + r, 4), 128)], cotg[r, :, slab(y, 512)], 1, 0) for r in range(4)]
-    gab[1] = (parts_b[0] + parts_b[1]) + (parts_b[2] + parts_b[3])
-    push("sb", (0,), gab.at[1 - c], sibin, sib)
-
-    for j in range(CHUNKS):
-        step_z(4, j)
-
-    def weight(j):
-        arrive("ws", (j, 0), part(z, 1 - c, j))
-        for k in (0, 1):
-            for s in range(1, HOPS[j % 2][k] + 1):
-                arrive("ws", (j, s if k == 0 else 4 + s), part(origin(k, s), 1 - c, j))
+    step_z(4, 0)
+    step_z(4, 1)
+    for u in range(2, 6):
+        step_z(2, u)
+    step_z(3, 2)
+    step_z(3, 3)
 
     up1, up2, up3 = (slab(lax.rem(y + d, 4), 128) for d in (1, 2, 3))
 
@@ -249,41 +255,6 @@
     def block(yy):
         return gb.at[eight, pl.ds(pl.multiple_of(x * 2048 + yy * 512, 512), 512)]
 
-    arrive("sb", (0,))
-    zin[z] = gab[c] + sibin[...]
-    for d in range(1, 8):
-        push("z", (d,), zin.at[z], zin.at[z], zed(d))
-    ld_w.wait()
-    for j in range(CHUNKS):
-        weight(j)
-    backward(2)
-    spread_end("t")
-    forward(0)
-    backward(1)
-    backward(3)
-    forward(1)
-    backward_on(0)
-    backward_on(1)
-    forward_on(0)
-    for d in range(1, 8):
-        arrive("z", (d,), zin.at[lax.rem(z + 8 - d, 8)])
-    total = zin[0]
-    for i in range(1, 8):
-        total = total + zin[i]
-    gav[c] = total * FACTOR
-    push("sb", (1,), gav.at[c], gav.at[c], sib)
-    forward(2)
-    arrive("sb", (1,), gav.at[1 - c])
-    ga_out = local(gav.at[0], ga)
-    for d in (1, 2, 3):
-        push("gy", (d,), gav.at[1, eight, :], block(y), col(d))
-    gb_own = local(gav.at[1, eight, :], block(y))
-    forward_on(1)
-    forward(3)
-    forward_on(2)
-    backward(0)
-    forward_on(3)
-
     def output(j):
         cols = pl.ds(j * CW, CW)
         for k in (0, 1):
@@ -297,16 +268,70 @@
             push("o2", (j, d), ob.at[slab(lax.rem(x + d, 4), 32), cols], out.at[:, here], row(d))
         return local(ob.at[slab(x, 32), cols], out.at[:, here])
 
+    ld_w.wait()
+    spread_end("c2")
+    weight(0, 1)
+    backward(2)
+    step_z(3, 4)
+    step_z(3, 5)
+
+    for d in (1, 2, 3):
+        arrive("ly", (d,))
+        arrive("lgy", (d,))
+    lowv[...] = ((ly[0] + ly[1]) + (ly[2] + ly[3])).astype(BF16)
+    parts_a = [dot(lgv[r], tokg[slab(lax.rem(y + r, 4), 128), pl.ds(0, 512)], 1, 0) for r in range(4)]
+    gab[0] = (parts_a[0] + parts_a[1]) + (parts_a[2] + parts_a[3])
+    parts_b = [dot(lowv[:, slab(lax.rem(y + r, 4), 128)], cotg[r, :, slab(y, 512)], 1, 0) for r in range(4)]
+    gab[1] = (parts_b[0] + parts_b[1]) + (parts_b[2] + parts_b[3])
+    push("sb", (0,), gab.at[1 - c], sibin, sib)
+    step_z(4, 2)
+    step_z(4, 3)
+    spread_end("t")
+    weight(2, 3)
+    forward(0)
+    step_z(4, 4)
+    step_z(4, 5)
+    arrive("sb", (0,))
+    zin[z] = gab[c] + sibin[...]
+    for d in range(1, 8):
+        push("z", (d,), zin.at[z], zin.at[z], zed(d))
+    forward(1)
+    forward_on(0)
+    weight(4, 5)
+    backward(1)
+    backward(3)
+    forward_on(1)
+    forward(2)
+    backward_on(0)
+    backward_on(1)
+    for d in range(1, 8):
+        arrive("z", (d,), zin.at[lax.rem(z + 8 - d, 8)])
+    total = zin[0]
+    for i in range(1, 8):
+        total = total + zin[i]
+    gav[c] = total * FACTOR
+    push("sb", (1,), gav.at[c], gav.at[c], sib)
+    own = [output(0)]
+    arrive("sb", (1,), gav.at[1 - c])
+    ga_out = local(gav.at[0], ga)
+    for d in (1, 2, 3):
+        push("gy", (d,), gav.at[1, eight, :], block(y), col(d))
+    gb_own = local(gav.at[1, eight, :], block(y))
+    forward(3)
+    forward_on(2)
+    own.append(output(1))
+    forward_on(3)
+    backward(0)
     gb_own.wait()
     for d in (1, 2, 3):
         arrive("gy", (d,), block(lax.rem(y + 4 - d, 4)))
     for d in (1, 2, 3):
         push("gx", (d,), gb.at[eight, slab(x, 2048)], gb.at[eight, slab(x, 2048)], row(d))
-    own = [output(0), output(1), output(2)]
+    own.append(output(2))
+    own.append(output(3))
     for d in (1, 2, 3):
         arrive("gx", (d,), gb.at[eight, slab(lax.rem(x + 4 - d, 4), 2048)])
     push("sb", (2,), gb.at[eight, :], gb.at[eight, :], sib)
-    own.append(output(3))
 
     for h in range(2):
         cols = pl.ds(h * 256, 256)

time: 87.7 us -> 85.1 us (0.970)
  Pallas kernels: 86.9 us -> 84.3 us
    pallas_call x1, Pallas kernels: 84.7 us -> 82.1 us  [per_device(): pl.pallas_call(kernel, out_shape=results, in_specs=[any_] * 5, out_specs=...]
where the time goes in v3:
time: 85.1 us; the launch traced here: 85 us
  Pallas kernels  84.3 us (99%)
    pallas_call x1, Pallas kernels, per_device(): pl.pallas_call(kernel, out_shape=results, in_specs=[any_] * 5, out_specs=...  82.1 us
    pallas_call x1, Pallas kernels, per_device(): pl.pallas_call(finish, out_shape=results, in_specs=[any_] * 4, out_specs=...  2.26 us

profile of v3, /device:TPU:1, one launch (start us, length us, event | category | flops | bytes accessed | tf_op | source)
XLA Modules:
  0.0 85.0 jit_solution(1812735900906443254)
XLA Ops:
  0.6 82.1 %projection.1 = (bf16[32,8192]{1,0:T(8,128)(2,1)}, bf16[512,512]{1,0:T(8,128)(2,1)}, f32[16,512]{1,0:T(8,128)}, f32[16,8192]{1,0:T(8,128)}) custom-call(bf16[512,512]{1,0:T(8,128)(2,1)} %tok.1, bf16[512,8192]{1,0:T(8,128)(2,1)} %w.1, bf16[16,512]{1,0:T(8,128)(2,1)} %bitcast.2, bf16[16,8192]{1,0:T(8,128)(2,1)} %up.1, bf16[32,8192]{1,0:T(8,128)(2,1)} %cot.1), custom_call_target="tpu_custom_call" | custom-call | tf_op jit(solution)/shard_map/projection/pallas_call | solution.py:380
  82.7 2.3 %results.1 = (bf16[32,8192]{1,0:T(8,128)(2,1)}, bf16[512,512]{1,0:T(8,128)(2,1)}, f32[16,512]{1,0:T(8,128)}, f32[16,8192]{1,0:T(8,128)}) custom-call(bf16[32,8192]{1,0:T(8,128)(2,1)} %get-tuple-element.12.a, bf16[512,512]{1,0:T(8,128)(2,1)} %get-tuple-element.13.b, f32[16,512]{1,0:T(8,128)} %get-tuple-element.14.c, f32[16,8192]{1,0:T(8,128)} %get-tuple-element.15.d), custom_call_target="tpu_custom_call" | custom-call | tf_op jit(solution)/shard_map/results/pallas_call | solution.py:391

commit v4 on v3

--- a/solution.py
+++ b/solution.py
@@ -207,18 +207,17 @@
     up1, up2, up3 = (slab(lax.rem(y + d, 4), 128) for d in (1, 2, 3))
 
     def forward(j):
-        @pl.loop(0, 2)
-        def _(q):
-            cols = slab(j * 2 + q, 256)
+        lo, hi, mid = pl.ds(j * CW, 256), pl.ds(j * CW + 256, 256), pl.ds(j * 256, 256)
+        for cols in (lo, hi):
             acc = dot(tokg[...], wg[:, :, cols].reshape(2048, 256), 1, 0)
             of[:, cols] = acc
             os[:, cols] = acc.astype(BF16)
-
-        lo, hi, mid = pl.ds(j * CW, 256), pl.ds(j * CW + 256, 256), pl.ds(j * 256, 256)
-        push("om", (j, 0), os.at[up2, lo], om.at[0, :, mid], col(1))
-        push("om", (j, 1), os.at[up2, hi], om.at[1, :, mid], col(3))
-        push("o1", (j, 0, 1), os.at[up1, hi], orx.at[0, :, hi], col(1))
-        push("o1", (j, 1, 0), os.at[up3, lo], orx.at[1, :, lo], col(3))
+            if cols is lo:
+                push("om", (j, 0), os.at[up2, lo], om.at[0, :, mid], col(1))
+                push("o1", (j, 1, 0), os.at[up3, lo], orx.at[1, :, lo], col(3))
+            else:
+                push("om", (j, 1), os.at[up2, hi], om.at[1, :, mid], col(3))
+                push("o1", (j, 0, 1), os.at[up1, hi], orx.at[0, :, hi], col(1))
 
     def forward_on(j):
         lo, hi, mid = pl.ds(j * CW, 256), pl.ds(j * CW + 256, 256), pl.ds(j * 256, 256)

time: 85.1 us -> 85.1 us (level)
  no operation moved by 1% of the time
where the time goes in v4:
time: 85.1 us; the launch traced here: 85 us
  Pallas kernels  84.3 us (99%)
    pallas_call x1, Pallas kernels, per_device(): pl.pallas_call(kernel, out_shape=results, in_specs=[any_] * 5, out_specs=...  82.1 us
    pallas_call x1, Pallas kernels, per_device(): pl.pallas_call(finish, out_shape=results, in_specs=[any_] * 4, out_specs=...  2.26 us

profile of v4, /device:TPU:1, one launch (start us, length us, event | category | flops | bytes accessed | tf_op | source)
XLA Modules:
  0.0 85.0 jit_solution(17830772330976365541)
XLA Ops:
  0.6 82.1 %projection.1 = (bf16[32,8192]{1,0:T(8,128)(2,1)}, bf16[512,512]{1,0:T(8,128)(2,1)}, f32[16,512]{1,0:T(8,128)}, f32[16,8192]{1,0:T(8,128)}) custom-call(bf16[512,512]{1,0:T(8,128)(2,1)} %tok.1, bf16[512,8192]{1,0:T(8,128)(2,1)} %w.1, bf16[16,512]{1,0:T(8,128)(2,1)} %bitcast.2, bf16[16,8192]{1,0:T(8,128)(2,1)} %up.1, bf16[32,8192]{1,0:T(8,128)(2,1)} %cot.1), custom_call_target="tpu_custom_call" | custom-call | tf_op jit(solution)/shard_map/projection/pallas_call | solution.py:379
  82.7 2.3 %results.1 = (bf16[32,8192]{1,0:T(8,128)(2,1)}, bf16[512,512]{1,0:T(8,128)(2,1)}, f32[16,512]{1,0:T(8,128)}, f32[16,8192]{1,0:T(8,128)}) custom-call(bf16[32,8192]{1,0:T(8,128)(2,1)} %get-tuple-element.12.a, bf16[512,512]{1,0:T(8,128)(2,1)} %get-tuple-element.13.b, f32[16,512]{1,0:T(8,128)} %get-tuple-element.14.c, f32[16,8192]{1,0:T(8,128)} %get-tuple-element.15.d), custom_call_target="tpu_custom_call" | custom-call | tf_op jit(solution)/shard_map/results/pallas_call | solution.py:390
